TPU v7x, 32 devices: a whole 2x2x4 slice. The times are simulated.
32 devices in a mesh: face: 4 (over z), tile: 8 (over y, x, core).
Axes of the slice: x: 2, y: 2, z: 4, core: 2. Of those that a mesh axis runs over, the one named last changes fastest.
Arguments:
- tracers: float32 [16, 32, 16, 1280], P('face', 'tile'), may hold values from -6 to 6
- basis_weights: float32 [2, 16, 32, 16, 16], P(None, 'face', 'tile'), may hold values from -1 to 1
- up_owner: int32 [2, 16, 32], P(None, 'face', 'tile'), may hold values from 0 to 4, as said below
- up_slot: int32 [2, 16, 32], P(None, 'face', 'tile'), may hold values from 0 to 15, as said below
- send_list: int32 [2, 16, 32], replicated, may hold values from 0 to 15, as said below
Outputs:
- transported: float32 [16, 32, 16, 1280], P('face', 'tile')
Inputs may be any that keep to these rules, and one draw needn't show every extreme that they name: `up_owner`: 0: the upstream element is on the same device; 1 and 2: on the device before or after along face, cyclically; 3 and 4: before or after along tile. On one device in one step, each position of each neighbour's list toward it is named by at most one target element, and a device names positions 0 to k - 1 of a list, k between 1 and 4, with 4 reached in every draw. `up_slot`: below 4 where up_owner is not 0. `send_list`: entry [s, 4 f + j, 4 t + c] is the c-th local element that device (f, t) lists in step s for direction j (j = 0: toward face + 1, 1: toward face - 1, 2: toward tile + 1, 3: toward tile - 1); the entries of one list are distinct.
All inputs are finite; a program needn't handle non-finite values.
Results may differ from a plain program's by a relative error of at most 0.0001.
Values sent between devices are 32-bit elements; how exact they have to be, the bound alone decides.
A program may use at most 64 MiB of HBM per device.

v0:
```python
import functools

import jax
import jax.numpy as jnp
from jax import lax
from jax.experimental import pallas as pl
from jax.experimental.pallas import tpu as pltpu
from jax.sharding import PartitionSpec as P

MESH = pl.DeviceIdType.MESH
NODES = 16
AHEAD = 3
HIGHEST = lax.Precision.HIGHEST


def chunk_width(columns):
    for width in (256, 128):
        if columns % width == 0:
            return width
    return columns


def halves(values):
    high = values.astype(jnp.bfloat16)
    return high, (values - high.astype(jnp.float32)).astype(jnp.bfloat16)


def kernel(dims, *refs):
    steps, side, cap, chunks, width = dims
    elems = side * side
    rows = elems * NODES
    operands, out, scratch = refs[:5], refs[5], refs[6:]
    (fields, weights, owners, slots, lists, load_sems, received, arrived, sending, mixing,
     source, moved, tile_out, tile_in, face_out, face_in,
     list_send, list_recv, tile_send, tile_recv, face_send, face_recv) = scratch
    loads = [
        pltpu.make_async_copy(
            operands[0].at[:, :, pl.ds(c * width, width)], fields.at[0, c], load_sems.at[4 + c]
        )
        for c in range(chunks)
    ]
    loads += [
        pltpu.make_async_copy(operands[1 + k], ref, load_sems.at[k])
        for k, ref in enumerate((weights, owners, slots, lists))
    ]
    for load in loads:
        load.start()

    face, tile = lax.axis_index("face"), lax.axis_index("tile")
    n_face, n_tile = lax.axis_size("face"), lax.axis_size("tile")
    south = (lax.rem(face + 1, n_face), tile)
    north = (lax.rem(face + n_face - 1, n_face), tile)
    east = (face, lax.rem(tile + 1, n_tile))
    west = (face, lax.rem(tile + n_tile - 1, n_tile))
    toward = (south, north, east, west)

    barrier = pltpu.get_barrier_semaphore()
    for device in toward:
        pl.semaphore_signal(barrier, inc=1, device_id=device, device_id_type=MESH)
    pl.semaphore_wait(barrier, 4)
    for load in loads:
        load.wait()

    def store(c):
        return pltpu.make_async_copy(
            moved.at[c],
            out.at[:, :, pl.ds(pl.multiple_of(c * width, width), width)],
            load_sems.at[4 + chunks + c],
        )

    def list_copy(s, c, j):
        return pltpu.make_async_remote_copy(
            src_ref=sending.at[s, c, j],
            dst_ref=received.at[s, c, j],
            send_sem=list_send.at[s, c, j],
            recv_sem=list_recv.at[s, c, j],
            device_id=toward[j],
            device_id_type=MESH,
        )

    def edge_copy(s, c, j):
        store, land, send, recv = (
            (tile_out, tile_in, tile_send, tile_recv)
            if j >= 2
            else (face_out, face_in, face_send, face_recv)
        )
        return pltpu.make_async_remote_copy(
            src_ref=store.at[s, c, j % 2],
            dst_ref=land.at[s, c, j % 2],
            send_sem=send.at[s, c, j % 2],
            recv_sem=recv.at[s, c, j % 2],
            device_id=toward[j],
            device_id_type=MESH,
        )

    def send_lists(s, c):
        for j in range(4):
            def pick(k, carry, j=j):
                elem = lists[s, 4 * face + j, tile * cap + k]
                sending[s, c, j, k] = fields[s, c, elem]
                return carry
            lax.fori_loop(0, cap, pick, 0, unroll=True)
            list_copy(s, c, j).start()

    def send_first(c, carry):
        send_lists(0, c)
        return carry

    ahead = min(AHEAD, chunks)
    lax.fori_loop(0, ahead, send_first, 0)

    lane = lax.broadcasted_iota(jnp.int32, (NODES, rows), 1)
    spread = jnp.where(
        (lane & (NODES - 1)) == lax.broadcasted_iota(jnp.int32, (NODES, rows), 0), 1.0, 0.0
    ).astype(jnp.float32)
    same = (lax.broadcasted_iota(jnp.int32, (rows, rows), 0) // NODES) == (
        lax.broadcasted_iota(jnp.int32, (rows, rows), 1) // NODES
    )
    def build(s, carry):
        repeated = jnp.dot(
            weights[s], spread, precision=HIGHEST, preferred_element_type=jnp.float32
        )
        high, low = halves(jnp.where(same, repeated, 0.0))
        mixing[s] = jnp.concatenate([high, low, high], axis=1)
        return carry

    lax.fori_loop(0, steps, build, 0)

    node = lax.broadcasted_iota(jnp.int32, (NODES, width), 0)
    flat_node = lax.broadcasted_iota(jnp.int32, (rows, width), 0) & (NODES - 1)

    def shift(block, amount):
        amount = amount % block.shape[0]
        return pltpu.roll(block, amount, 0) if amount else block

    def grid_of(flat):
        return flat.reshape(side, side, NODES, width)

    def pack(blocks, shifts, place):
        packed = shift(blocks[0], shifts[0])
        for k in range(1, side):
            packed = jnp.where(place == k, shift(blocks[k], shifts[k]), packed)
        return packed

    def interpolate(s, c):
        for j in range(4):
            list_copy(s, c, j).wait_recv()

        @pl.when((s == 0) & (c + ahead < chunks))
        def _():
            send_lists(0, c + ahead)

        arrived[...] = received[s, c]

        def pick(elem, carry):
            owner = owners[s, elem // side, elem % side]
            slot = slots[s, elem // side, elem % side]
            own = fields[s, c, slot]
            other = arrived[jnp.maximum(owner - 1, 0), jnp.minimum(slot, cap - 1)]
            source[elem] = jnp.where(owner == 0, own, other)
            return carry

        lax.fori_loop(0, elems, pick, 0, unroll=True)
        blocks = source[...]
        high, low = halves(blocks.reshape(rows, width))
        mixed = jnp.dot(
            mixing[s],
            jnp.concatenate([high, high, low], axis=0),
            preferred_element_type=jnp.float32,
        ).reshape(elems, NODES, width)
        mixed = jnp.clip(
            mixed, jnp.min(blocks, axis=1, keepdims=True), jnp.max(blocks, axis=1, keepdims=True)
        )
        moved[c] = mixed
        grid = mixed.reshape(side, side, NODES, width)
        place = node & 3
        tile_out[s, c, 0] = pack(
            [grid[x, side - 1] for x in range(side)], [x - 3 for x in range(side)], place
        )
        tile_out[s, c, 1] = pack([grid[x, 0] for x in range(side)], list(range(side)), place)
        edge_copy(s, c, 2).start()
        edge_copy(s, c, 3).start()

    def average(flat, before, after, low, high, hop):
        return jnp.where(
            low,
            0.5 * (flat + shift(before, -hop)),
            jnp.where(high, 0.5 * (flat + shift(after, hop)), flat),
        )

    def average_columns(s, c):
        edge_copy(s, c, 2).wait_recv()
        edge_copy(s, c, 3).wait_recv()
        flat = moved[c].reshape(rows, width)
        grid = grid_of(flat)
        from_west, from_east = tile_in[s, c, 0], tile_in[s, c, 1]
        left = jnp.stack([shift(from_west, 3 - x) for x in range(side)])[:, None]
        right = jnp.stack([shift(from_east, -x) for x in range(side)])[:, None]
        before = jnp.concatenate([left, grid[:, : side - 1]], axis=1).reshape(rows, width)
        after = jnp.concatenate([grid[:, 1:], right], axis=1).reshape(rows, width)
        flat = average(flat, before, after, (flat_node & 3) == 0, (flat_node & 3) == 3, 3)
        moved[c] = flat.reshape(elems, NODES, width)
        grid = grid_of(flat)
        place = node >> 2
        face_out[s, c, 0] = pack(
            [grid[side - 1, y] for y in range(side)], [4 * y - 12 for y in range(side)], place
        )
        face_out[s, c, 1] = pack(
            [grid[0, y] for y in range(side)], [4 * y for y in range(side)], place
        )
        edge_copy(s, c, 0).start()
        edge_copy(s, c, 1).start()

    def average_rows(s, c):
        edge_copy(s, c, 0).wait_recv()
        edge_copy(s, c, 1).wait_recv()
        flat = moved[c].reshape(rows, width)
        grid = grid_of(flat)
        from_north, from_south = face_in[s, c, 0], face_in[s, c, 1]
        above = jnp.stack([shift(from_north, 12 - 4 * y) for y in range(side)])[None]
        below = jnp.stack([shift(from_south, -4 * y) for y in range(side)])[None]
        before = jnp.concatenate([above, grid[: side - 1]], axis=0).reshape(rows, width)
        after = jnp.concatenate([grid[1:], below], axis=0).reshape(rows, width)
        flat = average(flat, before, after, flat_node < 4, flat_node >= 12, 12)
        averaged = flat.reshape(elems, NODES, width)

        @pl.when(s < steps - 1)
        def _():
            fields[s + 1, c] = averaged
            send_lists(s + 1, c)

        @pl.when(s == steps - 1)
        def _():
            moved[c] = averaged
            store(c).start()

    phases = (interpolate, average_columns, average_rows)
    def advance(turn, carry):
        def advance_step(s, carry):
            for phase in (2, 1, 0):
                c = turn - chunks * (3 * s + phase)

                @pl.when((c >= 0) & (c < chunks))
                def _():
                    phases[phase](s, c)

            return carry

        return lax.fori_loop(0, steps, advance_step, carry)

    lax.fori_loop(0, chunks + chunks * (3 * steps - 1), advance, 0)

    def finish(k, carry):
        s, c = k // chunks, k % chunks
        for j in range(4):
            list_copy(s, c, j).wait_send()
            edge_copy(s, c, j).wait_send()
        return carry

    lax.fori_loop(0, steps * chunks, finish, 0)

    def finish_store(c, carry):
        store(c).wait()
        return carry

    lax.fori_loop(0, chunks, finish_store, 0)


def local(tracers, basis_weights, up_owner, up_slot, send_list):
    side = tracers.shape[0]
    columns = tracers.shape[3]
    steps = basis_weights.shape[0]
    elems = side * side
    rows = elems * NODES
    cap = send_list.shape[2] // lax.axis_size("tile")
    width = chunk_width(columns)
    chunks = columns // width
    dims = (steps, side, cap, chunks, width)
    whole = pl.BlockSpec(memory_space=pltpu.HBM)
    f32 = jnp.float32
    edges = pltpu.VMEM((steps, chunks, 2, NODES, width), f32)
    list_sems = pltpu.SemaphoreType.DMA((steps, chunks, 4))
    edge_sems = pltpu.SemaphoreType.DMA((steps, chunks, 2))
    result = pl.pallas_call(
        functools.partial(kernel, dims),
        out_shape=jax.ShapeDtypeStruct((elems, NODES, columns), f32),
        in_specs=[whole] * 5,
        out_specs=whole,
        scratch_shapes=[
            pltpu.VMEM((steps, chunks, elems, NODES, width), f32),
            pltpu.VMEM((steps, rows, NODES), f32),
            pltpu.SMEM(up_owner.shape, jnp.int32),
            pltpu.SMEM(up_slot.shape, jnp.int32),
            pltpu.SMEM(send_list.shape, jnp.int32),
            pltpu.SemaphoreType.DMA((4 + 2 * chunks,)),
            pltpu.VMEM((steps, chunks, 4, cap, NODES, width), f32),
            pltpu.VMEM((4, cap, NODES, width), f32),
            pltpu.VMEM((steps, chunks, 4, cap, NODES, width), f32),
            pltpu.VMEM((steps, rows, 3 * rows), jnp.bfloat16),
            pltpu.VMEM((elems, NODES, width), f32),
            pltpu.VMEM((chunks, elems, NODES, width), f32),
            edges,
            edges,
            edges,
            edges,
            list_sems,
            list_sems,
            edge_sems,
            edge_sems,
            edge_sems,
            edge_sems,
        ],
        compiler_params=pltpu.CompilerParams(
            collective_id=0, has_side_effects=True, vmem_limit_bytes=62 * 1024 * 1024
        ),
        cost_estimate=pl.CostEstimate(
            flops=2 * steps * rows * NODES * columns,
            bytes_accessed=8 * rows * columns,
            transcendentals=0,
        ),
    )(
        tracers.reshape(elems, NODES, columns),
        basis_weights.reshape(steps, rows, NODES),
        up_owner,
        up_slot,
        send_list,
    )
    return result.reshape(side, side, NODES, columns)


def solution(mesh):
    return jax.shard_map(
        local,
        mesh=mesh,
        in_specs=(
            P("face", "tile", None, None),
            P(None, "face", "tile", None, None),
            P(None, "face", "tile"),
            P(None, "face", "tile"),
            P(),
        ),
        out_specs=P("face", "tile", None, None),
        check_vma=False,
    )
```

profile of v0, /device:TPU:0, one launch (start us, length us, event | category | flops | bytes accessed | tf_op | source)
XLA Modules:
  0.0 52.3 jit_solution(4483255332835523066)
XLA Ops:
  0.0 49.8 %shard_map.55 = f32[16,16,1280]{2,1,0:T(8,128)} custom-call(f32[16,16,1280]{2,1,0:T(8,128)} %bitcast.4, f32[2,256,16]{2,1,0:T(8,128)} %bitcast.5, s32[2,4,4]{2,1,0:T(4,128)} %refs_2_.1, s32[2,4,4]{2,1,0:T(4,128)} %refs_3_.1, s32[2,16,32]{2,1,0:T(8,128)} %refs_4_.1), custom_call_target="tpu_custom_call" | custom-call | flops 20971520 | bytes 2621440 | tf_op jit(solution)/shard_map/pallas_call | solution.py:284
  49.8 2.5 %copy.7 = f32[4,4,16,1280]{3,2,1,0:T(8,128)} copy(f32[4,4,16,1280]{3,2,1,0:T(8,128)} %bitcast.3) | data formatting | bytes 2621440
where the time goes:
time: 52.4 us; the launch traced here: 52.3 us
  Pallas kernels  49.8 us (95%)
  local copies, waits for them, and re-layouts  2.47 us (5%)
    pallas_call x1, Pallas kernels, local(): pl.pallas_call(functools.partial(kernel, dims), out_shape=jax.ShapeDtypeS...  49.8 us
    unnamed x1, local copies, waits for them, and re-layouts  2.47 us

commit v1 on v0

--- a/solution.py
+++ b/solution.py
@@ -31,7 +31,7 @@
     rows = elems * NODES
     operands, out, scratch = refs[:5], refs[5], refs[6:]
     (fields, weights, owners, slots, lists, load_sems, received, arrived, sending, mixing,
-     source, moved, tile_out, tile_in, face_out, face_in,
+     source, tile_out, tile_in, face_out, face_in,
      list_send, list_recv, tile_send, tile_recv, face_send, face_recv) = scratch
     loads = [
         pltpu.make_async_copy(
@@ -63,7 +63,7 @@
 
     def store(c):
         return pltpu.make_async_copy(
-            moved.at[c],
+            fields.at[steps, c],
             out.at[:, :, pl.ds(pl.multiple_of(c * width, width), width)],
             load_sems.at[4 + chunks + c],
         )
@@ -171,8 +171,21 @@
         mixed = jnp.clip(
             mixed, jnp.min(blocks, axis=1, keepdims=True), jnp.max(blocks, axis=1, keepdims=True)
         )
-        moved[c] = mixed
         grid = mixed.reshape(side, side, NODES, width)
+        left = jnp.stack([shift(grid[x, 0], 3) for x in range(side)])[:, None]
+        right = jnp.stack([shift(grid[x, side - 1], -3) for x in range(side)])[:, None]
+        before = jnp.concatenate([left, grid[:, : side - 1]], axis=1).reshape(rows, width)
+        after = jnp.concatenate([grid[:, 1:], right], axis=1).reshape(rows, width)
+        flat = mixed.reshape(rows, width)
+        flat = average(flat, before, after, (flat_node & 3) == 0, (flat_node & 3) == 3, 3)
+        grid = grid_of(flat)
+        above = jnp.stack([shift(grid[0, y], 12) for y in range(side)])[None]
+        below = jnp.stack([shift(grid[side - 1, y], -12) for y in range(side)])[None]
+        before = jnp.concatenate([above, grid[: side - 1]], axis=0).reshape(rows, width)
+        after = jnp.concatenate([grid[1:], below], axis=0).reshape(rows, width)
+        flat = average(flat, before, after, flat_node < 4, flat_node >= 12, 12)
+        grid = grid_of(flat)
+        fields[s + 1, c] = flat.reshape(elems, NODES, width)
         place = node & 3
         tile_out[s, c, 0] = pack(
             [grid[x, side - 1] for x in range(side)], [x - 3 for x in range(side)], place
@@ -188,25 +201,24 @@
             jnp.where(high, 0.5 * (flat + shift(after, hop)), flat),
         )
 
+    def blend(s, c, elem, beside, where):
+        block = fields[s + 1, c, elem]
+        fields[s + 1, c, elem] = jnp.where(where, 0.5 * (block + beside), block)
+
     def average_columns(s, c):
         edge_copy(s, c, 2).wait_recv()
         edge_copy(s, c, 3).wait_recv()
-        flat = moved[c].reshape(rows, width)
-        grid = grid_of(flat)
         from_west, from_east = tile_in[s, c, 0], tile_in[s, c, 1]
-        left = jnp.stack([shift(from_west, 3 - x) for x in range(side)])[:, None]
-        right = jnp.stack([shift(from_east, -x) for x in range(side)])[:, None]
-        before = jnp.concatenate([left, grid[:, : side - 1]], axis=1).reshape(rows, width)
-        after = jnp.concatenate([grid[:, 1:], right], axis=1).reshape(rows, width)
-        flat = average(flat, before, after, (flat_node & 3) == 0, (flat_node & 3) == 3, 3)
-        moved[c] = flat.reshape(elems, NODES, width)
-        grid = grid_of(flat)
+        for x in range(side):
+            blend(s, c, x * side, shift(from_west, -x), (node & 3) == 0)
+            blend(s, c, x * side + side - 1, shift(from_east, 3 - x), (node & 3) == 3)
         place = node >> 2
         face_out[s, c, 0] = pack(
-            [grid[side - 1, y] for y in range(side)], [4 * y - 12 for y in range(side)], place
+            [fields[s + 1, c, (side - 1) * side + y] for y in range(side)],
+            [4 * y - 12 for y in range(side)], place
         )
         face_out[s, c, 1] = pack(
-            [grid[0, y] for y in range(side)], [4 * y for y in range(side)], place
+            [fields[s + 1, c, y] for y in range(side)], [4 * y for y in range(side)], place
         )
         edge_copy(s, c, 0).start()
         edge_copy(s, c, 1).start()
@@ -214,24 +226,17 @@
     def average_rows(s, c):
         edge_copy(s, c, 0).wait_recv()
         edge_copy(s, c, 1).wait_recv()
-        flat = moved[c].reshape(rows, width)
-        grid = grid_of(flat)
         from_north, from_south = face_in[s, c, 0], face_in[s, c, 1]
-        above = jnp.stack([shift(from_north, 12 - 4 * y) for y in range(side)])[None]
-        below = jnp.stack([shift(from_south, -4 * y) for y in range(side)])[None]
-        before = jnp.concatenate([above, grid[: side - 1]], axis=0).reshape(rows, width)
-        after = jnp.concatenate([grid[1:], below], axis=0).reshape(rows, width)
-        flat = average(flat, before, after, flat_node < 4, flat_node >= 12, 12)
-        averaged = flat.reshape(elems, NODES, width)
+        for y in range(side):
+            blend(s, c, y, shift(from_north, -4 * y), node < 4)
+            blend(s, c, (side - 1) * side + y, shift(from_south, 12 - 4 * y), node >= 12)
 
         @pl.when(s < steps - 1)
         def _():
-            fields[s + 1, c] = averaged
             send_lists(s + 1, c)
 
         @pl.when(s == steps - 1)
         def _():
-            moved[c] = averaged
             store(c).start()
 
     phases = (interpolate, average_columns, average_rows)
@@ -287,7 +292,7 @@
         in_specs=[whole] * 5,
         out_specs=whole,
         scratch_shapes=[
-            pltpu.VMEM((steps, chunks, elems, NODES, width), f32),
+            pltpu.VMEM((steps + 1, chunks, elems, NODES, width), f32),
             pltpu.VMEM((steps, rows, NODES), f32),
             pltpu.SMEM(up_owner.shape, jnp.int32),
             pltpu.SMEM(up_slot.shape, jnp.int32),
@@ -298,7 +303,6 @@
             pltpu.VMEM((steps, chunks, 4, cap, NODES, width), f32),
             pltpu.VMEM((steps, rows, 3 * rows), jnp.bfloat16),
             pltpu.VMEM((elems, NODES, width), f32),
-            pltpu.VMEM((chunks, elems, NODES, width), f32),
             edges,
             edges,
             edges,

time: 52.4 us -> 52.5 us (level)
  no operation moved by 1% of the time
where the time goes in v1:
time: 52.5 us; the launch traced here: 52.4 us
  Pallas kernels  49.9 us (95%)
  local copies, waits for them, and re-layouts  2.47 us (5%)
    pallas_call x1, Pallas kernels, local(): pl.pallas_call(functools.partial(kernel, dims), out_shape=jax.ShapeDtypeS...  49.9 us
    unnamed x1, local copies, waits for them, and re-layouts  2.47 us

profile of v1, /device:TPU:0, one launch (start us, length us, event | category | flops | bytes accessed | tf_op | source)
XLA Modules:
  0.0 52.4 jit_solution(10887525955702656888)
XLA Ops:
  0.0 49.9 %shard_map.55 = f32[16,16,1280]{2,1,0:T(8,128)} custom-call(f32[16,16,1280]{2,1,0:T(8,128)} %bitcast.4, f32[2,256,16]{2,1,0:T(8,128)} %bitcast.5, s32[2,4,4]{2,1,0:T(4,128)} %refs_2_.1, s32[2,4,4]{2,1,0:T(4,128)} %refs_3_.1, s32[2,16,32]{2,1,0:T(8,128)} %refs_4_.1), custom_call_target="tpu_custom_call" | custom-call | flops 20971520 | bytes 2621440 | tf_op jit(solution)/shard_map/pallas_call | solution.py:289
  49.9 2.5 %copy.7 = f32[4,4,16,1280]{3,2,1,0:T(8,128)} copy(f32[4,4,16,1280]{3,2,1,0:T(8,128)} %bitcast.3) | data formatting | bytes 2621440
